TPU v7x, 32 devices: a whole 2x2x4 slice. The times are simulated.
32 devices in a mesh: grp: 2 (over y), sp: 4 (over z), ch: 2 (over x), sub: 2 (over core).
Axes of the slice: x: 2, y: 2, z: 4, core: 2. Of those that a mesh axis runs over, the one named last changes fastest.
Arguments:
- volume: bfloat16 [64, 32, 64, 128], P('ch', ('grp', 'sp'), 'sub'), parts along dimension 1, may hold values from -6 to 6
- kernel: bfloat16 [128, 64, 64], P(None, 'ch'), may hold values from -0.09375 to 0.09375
- cotangent: bfloat16 [128, 16, 2048], P('ch', ('grp', 'sp'), 'sub'), parts along dimension 1, may hold values from -6 to 6
Outputs:
- features: bfloat16 [128, 16, 2048], P('ch', ('grp', 'sp'), 'sub'), parts along dimension 1
- volume_grad: bfloat16 [64, 32, 64, 128], P('ch', ('grp', 'sp'), 'sub'), parts along dimension 1
- kernel_grad: float32 [256, 64, 64], P(('grp', 'sp', 'sub'), 'ch'), parts along dimension 0
There are 2 independent parts, one for each index of `grp`. A program takes and returns all parts, laid end to end along the dimension named above; an argument that names none is the same for every part. Nothing has to cross between parts.
All inputs are finite; a program needn't handle non-finite values.
Results may differ from a plain program's by a relative error of at most 0.0034.
Values may be sent and summed in bfloat16 or wider, within the bound.
A program may use at most 128 MiB of HBM per device.

v0:
```python
import jax
import jax.numpy as jnp
from jax import lax
from jax.sharding import PartitionSpec as P


def padded_2(cells, sides, width):
    for axis, dim in sides:
        count = lax.axis_size(axis)
        ends = count - 1
        head = lax.slice_in_dim(cells, 0, width, axis=dim)
        tail = lax.slice_in_dim(cells, cells.shape[dim] - width, cells.shape[dim], axis=dim)
        cells = jnp.concatenate(
            [
                lax.ppermute(tail, axis, [(i, (i + 1) % count) for i in range(ends)]),
                cells,
                lax.ppermute(head, axis, [((i + 1) % count, i) for i in range(ends)]),
            ],
            axis=dim,
        )
    return cells


def strided(padded, filters):
    result = lax.conv_general_dilated(
        padded[None],
        filters,
        (2, 2, 2),
        ((0, 0), (0, 0), (1, 1)),
        dimension_numbers=("NCDHW", "OIDHW", "NCDHW"),
        preferred_element_type=jnp.float32,
    )
    return result[0]


def body(volume, kernel, cotangent):
    n_out = kernel.shape[0]
    local_in = kernel.shape[1]
    padded = padded_2(volume, (("sp", 1), ("sub", 2)), 1)
    filters = kernel.reshape(n_out, local_in, 4, 4, 4)
    out_depth = volume.shape[1] // 2
    out_high = volume.shape[2] // 2
    out_wide = volume.shape[3] // 2
    local_out = n_out // lax.axis_size("ch")
    summed = lax.psum_scatter(
        strided(padded, filters).reshape(
            local_out * lax.axis_size("ch"), out_depth, out_high * out_wide
        ),
        "ch",
        scatter_dimension=0,
        tiled=True,
    )
    features = summed.astype(jnp.bfloat16)
    local_grad = cotangent.reshape(local_out, out_depth, out_high, out_wide)
    gathered = lax.all_gather(local_grad, "ch", axis=0, tiled=True)
    grad_rims = padded_2(gathered, (("sp", 1), ("sub", 2)), 1)
    flipped = jnp.flip(filters, (2, 3, 4)).transpose(1, 0, 2, 3, 4)
    volume_grad = lax.conv_general_dilated(
        grad_rims[None],
        flipped,
        (1, 1, 1),
        ((0, 0), (0, 0), (2, 2)),
        lhs_dilation=(2, 2, 2),
        dimension_numbers=("NCDHW", "OIDHW", "NCDHW"),
        preferred_element_type=jnp.float32,
    )[0].astype(jnp.bfloat16)
    grad_core = grad_rims[:, 1:-1, 1:-1, :]
    filter_term = lax.conv_general_dilated(
        padded[None],
        grad_core[None],
        (1, 1, 1),
        ((0, 0), (0, 0), (1, 1)),
        rhs_dilation=(2, 2, 2),
        dimension_numbers=("CNDHW", "IODHW", "NCDHW"),
        preferred_element_type=jnp.float32,
    )
    filter_term = filter_term.transpose(1, 0, 2, 3, 4).reshape(n_out, local_in, 64)
    kernel_grad = lax.psum_scatter(filter_term, ("sp", "sub"), scatter_dimension=0, tiled=True)
    return (features, volume_grad, kernel_grad)


def solution(mesh):
    return jax.shard_map(
        body,
        mesh=mesh,
        in_specs=(
            P("ch", ("grp", "sp"), "sub", None),
            P(None, "ch", None),
            P("ch", ("grp", "sp"), "sub"),
        ),
        out_specs=(
            P("ch", ("grp", "sp"), "sub"),
            P("ch", ("grp", "sp"), "sub", None),
            P(("grp", "sp", "sub"), "ch", None),
        ),
        check_vma=False,
    )
```

profile of v0, /device:TPU:0, one launch (start us, length us, event | category | flops | bytes accessed | tf_op | source)
XLA Modules:
  0.0 278.4 jit_solution(10113635710684621156)
XLA Ops:
  7.2 1.9 fusion.30
  9.1 5.6 %collective-permute-start = (bf16[32,1,32,128]{3,2,1,0:T(8,128)(2,1)}, bf16[32,1,32,128]{3,2,1,0:T(8,128)(2,1)}, u32[]{:S(2)}, u32[]{:S(2)}) collective-permute-start(bf16[32,1,32,128]{3,2,1,0:T(8,128)(2,1)} %get-tuple-element.24), channel_id=1, source_target_pairs={{0,4},{4,8},{8,12},{1,5},{5,9},{9,13},{2,6},{6,10},{10,14},{3,7},{... | collective-permute-start | bytes 786440 | tf_op jit(solution)/shard_map/ppermute | solution.py:15
  17.5 14.2 %all_gather.3 = bf16[128,2,16,64]{3,2,1,0:T(8,128)(2,1)S(1)} all-gather(bf16[64,2,16,64]{3,2,1,0:T(8,128)(2,1)S(1)} %reshape.17), channel_id=1, replica_groups=mesh['grp'=2,'sp'=4,'ch'=2,'sub'=2] {'ch'}, dimensions={0}, use_global_device_ids=true | all-gather | bytes 786432 | tf_op jit(solution)/shard_map/all_gather | solution.py:55
  32.9 5.0 %collective-permute-start.4 = (bf16[128,1,16,64]{3,2,1,0:T(8,128)(2,1)}, bf16[128,1,16,64]{3,2,1,0:T(8,128)(2,1)}, u32[]{:S(2)}, u32[]{:S(2)}) collective-permute-start(bf16[128,1,16,64]{3,2,1,0:T(8,128)(2,1)} %get-tuple-element.22), channel_id=1, source_target_pairs={{0,4},{4,8},{8,12},{1,5},{5,9},{9,13},{2,6},{6,10},{10,14},{3,7},{... | collective-permute-start | bytes 786440 | tf_op jit(solution)/shard_map/ppermute | solution.py:15
  39.2 2.3 copy.98
  45.3 3.0 %collective-permute-start.2 = (bf16[32,6,1,128]{3,0,2,1:T(8,128)(2,1)S(1)}, bf16[32,6,1,128]{3,0,2,1:T(8,128)(2,1)S(1)}, u32[]{:S(2)}, u32[]{:S(2)}) collective-permute-start(bf16[32,6,1,128]{3,0,2,1:T(8,128)(2,1)S(1)} %copy.105), channel_id=1, source_target_pairs={{0,1},{2,3},{4,5},{6,7},{8,9},{10,11},{12,13},{14,15},{16,17},{18,... | collective-permute-start | bytes 147464 | tf_op jit(solution)/shard_map/ppermute | solution.py:15
  49.7 2.2 collective-permute-done.5
  54.6 10.0 %copy.79 = bf16[32,6,32,128]{2,0,3,1:T(8,128)(2,1)} copy(bf16[32,6,32,128]{3,2,1,0:T(8,128)(2,1)} %copy-done.4) | data formatting | bytes 3145728 | tf_op jit(solution)/shard_map/concatenate | solution.py:13
  64.6 2.9 %copy.88 = bf16[128,4,16,64]{0,3,2,1:T(8,128)(2,1)} copy(bf16[128,4,16,64]{3,2,1,0:T(8,128)(2,1)S(1)} %copy-done.2) | data formatting | bytes 2097152 | tf_op jit(solution)/shard_map/concatenate | solution.py:13
  68.8 4.4 %collective-permute-start.6 = (bf16[128,4,1,64]{3,2,1,0:T(2,128)(2,1)}, bf16[128,4,1,64]{3,2,1,0:T(2,128)(2,1)}, u32[]{:S(2)}, u32[]{:S(2)}) collective-permute-start(bf16[128,4,1,64]{3,2,1,0:T(2,128)(2,1)} %get-tuple-element.17), channel_id=1, source_target_pairs={{0,1},{2,3},{4,5},{6,7},{8,9},{10,11},{12,13},{14,15},{16,17},{18,... | collective-permute-start | bytes 196616 | tf_op jit(solution)/shard_map/ppermute | solution.py:15
  73.3 9.7 %copy.80 = bf16[32,6,1,128]{2,0,3,1:T(8,128)(2,1)} copy(bf16[32,6,1,128]{3,0,2,1:T(8,128)(2,1)S(1)} %collective-permute-done.3) | data formatting | bytes 98304 | tf_op jit(solution)/shard_map/ppermute | solution.py:17
  82.9 9.7 %copy.78 = bf16[32,6,1,128]{2,0,3,1:T(8,128)(2,1)} copy(bf16[32,6,1,128]{3,0,2,1:T(8,128)(2,1)S(1)} %collective-permute-done.2) | data formatting | bytes 98304 | tf_op jit(solution)/shard_map/ppermute | solution.py:15
  92.6 12.4 %fusion.26 = (bf16[1,32,6,34,128]{3,1,4,2,0:T(8,128)(2,1)}, bf16[32,6,34,1,128]{2,0,4,1,3:T(8,128)(2,1)S(1)}) fusion(bf16[32,6,1,128]{2,0,3,1:T(8,128)(2,1)} %copy.80, bf16[32,6,32,128]{2,0,3,1:T(8,128)(2,1)} %copy.79, bf16[32,6,1,128]{2,0,3,1:T(8,128)(2,1)} %copy.78), kind=kLoop, calls=%fused_computation.36 | loop fusion | flops 5013504 | bytes 5013504 | tf_op jit(solution)/shard_map/broadcast_in_dim | solution.py:26
  105.0 4.2 %pad = bf16[32,6,34,1,144]{2,0,4,1,3:T(8,128)(2,1)} pad(bf16[32,6,34,1,128]{2,0,4,1,3:T(8,128)(2,1)S(1)} %get-tuple-element.16, bf16[]{:T(256)} %constant.2), padding=0_0x0_0x0_0x0_0x1_15 | pad | bytes 3551234 | tf_op jit(solution)/shard_map/broadcast_in_dim | solution.py:26
  109.3 12.6 %copy.82 = bf16[32,6,34,1,8,18]{0,4,5,2,1,3:T(8,128)(2,1)} copy(bf16[32,6,34,1,8,18]{2,0,5,4,1,3:T(8,128)(2,1)} %bitcast.33) | data formatting | bytes 3760128 | tf_op jit(solution)/shard_map/conv_general_dilated | solution.py:25
  123.6 8.3 %fusion.13 = f32[2,16,8,9,128]{4,2,3,1,0:T(8,128)S(1)} fusion(bf16[32,6,34,1,7,3]{0,4,5,2,1,3:T(8,128)(2,1)S(1)} %slice.38, bf16[32,6,34,1,8,18]{0,4,5,2,1,3:T(8,128)(2,1)} %copy.82, pred[8,9]{0,1:T(8,128)(4,1)S(1)} %copy-done.10, bf16[128,32,4,4,4]{0,4,3,2,1:T(4,128)(2,1)S(1)} %bitcast.31), kind=kOutput, calls=%fused_computation.16 | convolution fusion | flops 1214834688 | bytes 3858248 | tf_op jit(solution)/shard_map/conv_general_dilated | solution.py:25
  133.1 27.5 %all-reduce.2 = bf16[128,2,1024]{2,1,0:T(2,128)(2,1)} all-reduce(f32[128,2,1024]{2,1,0:T(2,128)S(1)} %copy.86), channel_id=2, replica_groups=mesh['grp'=2,'sp'=4,'ch'=2,'sub'=2] {'ch'}, use_global_device_ids=true, to_apply=%region_0.0.clone | all-reduce | flops 262144 | bytes 1572864
  160.6 28.7 %copy.97 = bf16[1,32,6,34,128]{1,0,4,3,2:T(2,128)(2,1)} copy(bf16[1,32,6,34,128]{3,1,4,2,0:T(8,128)(2,1)} %get-tuple-element.15) | data formatting | bytes 3342336 | tf_op jit(solution)/shard_map/broadcast_in_dim | solution.py:26
  189.3 45.0 %fusion.31 = f32[128,32,4,4,4]{0,1,4,3,2:T(8,128)S(1)} fusion(bf16[1,32,6,34,128]{1,0,4,3,2:T(2,128)(2,1)} %copy.97, bf16[1,128,2,16,64]{1,0,4,3,2:T(2,128)(2,1)S(1)} %copy-done.7), kind=kOutput, calls=%fused_computation.41 | convolution fusion | flops 1065353216 | bytes 3244032 | tf_op jit(solution)/shard_map/transpose | solution.py:77
  234.4 2.9 %copy.99 = f32[128,32,64]{2,1,0:T(8,128)} copy(f32[128,32,64]{0,1,2:T(8,128)S(1)} %bitcast.39) | data formatting | bytes 2097152 | tf_op jit(solution)/shard_map/reshape | solution.py:77
  242.4 10.4 %select_convert_fusion = bf16[4,32,8,18,32]{4,2,3,1,0:T(8,128)(2,1)S(1)} fusion(pred[8,18]{0,1:T(8,128)(4,1)S(1)} %copy-done.9, bf16[128,4,18,1,7,2]{0,4,5,2,1,3:T(8,128)(2,1)S(1)} %slice.44, bf16[128,4,18,1,8,9]{0,4,5,2,1,3:T(8,128)(2,1)S(1)} %copy.92, bf16[128,32,4,4,4]{0,4,3,2,1:T(4,128)(2,1)S(1)} %bitcast.32), kind=kOutput, calls=%fused_computation.2 | convolution fusion | flops 1214005248 | bytes 3289232 | tf_op jit(solution)/shard_map/conv_general_dilated | solution.py:58
  254.0 2.7 slice_bitcast_fusion
  256.7 7.6 %copy.100 = bf16[32,4,32,128]{3,2,1,0:T(8,128)(2,1)} copy(bf16[32,4,32,128]{0,2,3,1:T(8,128)(2,1)} %slice_bitcast_fusion) | data formatting | bytes 2097152
  264.3 7.3 %reduce-scatter.2.cloned.1.call-done = f32[16,32,64]{2,1,0:T(8,128)} async-done(((f32[128,32,64]{2,1,0:T(8,128)}), f32[16,32,64]{2,1,0:T(8,128)}) %reduce-scatter.2.cloned.1.call-update) | async-done | bytes 131088 | tf_op jit(solution)/shard_map/reduce_scatter | solution.py:78
  (62 shorter events, 22.8 us)
Async XLA Ops:
  7.2 116.4 %copy-start = (bf16[128,32,64]{0,2,1:T(8,128)(2,1)S(1)}, bf16[128,32,64]{0,2,1:T(8,128)(2,1)}, u32[]{:S(2)}) copy-start(bf16[128,32,64]{0,2,1:T(8,128)(2,1)} %param.4) | copy-start | bytes 1572868
  7.2 264.4 %reduce-scatter.2.cloned.1.call-start = ((), (), s32[]{:S(2)}) async-start(), calls=%async_computation.1 | async-start | bytes 2359296 | tf_op jit(solution)/shard_map/reduce_scatter | solution.py:78
  9.1 33.5 %collective-permute-start = (bf16[32,1,32,128]{3,2,1,0:T(8,128)(2,1)}, bf16[32,1,32,128]{3,2,1,0:T(8,128)(2,1)}, u32[]{:S(2)}, u32[]{:S(2)}) collective-permute-start(bf16[32,1,32,128]{3,2,1,0:T(8,128)(2,1)} %get-tuple-element.24), channel_id=1, source_target_pairs={{0,4},{4,8},{8,12},{1,5},{5,9},{9,13},{2,6},{6,10},{10,14},{3,7},{... | collective-permute-start | bytes 786440 | tf_op jit(solution)/shard_map/ppermute | solution.py:15
  14.8 26.7 %copy-start.8 = (u32[32]{0:T(128)S(1)}, u32[32]{0:T(128)}, u32[]{:S(2)}) copy-start(u32[32]{0:T(128)} %constant.14) | copy-start | bytes 388
  14.8 29.0 %collective-permute-start.1 = (bf16[32,1,32,128]{3,2,1,0:T(8,128)(2,1)}, bf16[32,1,32,128]{3,2,1,0:T(8,128)(2,1)S(1)}, u32[]{:S(2)}, u32[]{:S(2)}) collective-permute-start(bf16[32,1,32,128]{3,2,1,0:T(8,128)(2,1)} %get-tuple-element.23), channel_id=1, source_target_pairs={{4,0},{8,4},{12,8},{5,1},{9,5},{13,9},{6,2},{10,6},{14,10},{7,3},{... | collective-permute-start | bytes 786440 | tf_op jit(solution)/shard_map/ppermute | solution.py:17
  17.5 26.1 %copy-start.5 = (bf16[32,4,32,128]{3,2,1,0:T(8,128)(2,1)S(1)}, bf16[32,4,32,128]{3,2,1,0:T(8,128)(2,1)}, u32[]{:S(2)}) copy-start(bf16[32,4,32,128]{3,2,1,0:T(8,128)(2,1)} %param.3) | copy-start | bytes 3145732
  32.9 15.5 %collective-permute-start.4 = (bf16[128,1,16,64]{3,2,1,0:T(8,128)(2,1)}, bf16[128,1,16,64]{3,2,1,0:T(8,128)(2,1)}, u32[]{:S(2)}, u32[]{:S(2)}) collective-permute-start(bf16[128,1,16,64]{3,2,1,0:T(8,128)(2,1)} %get-tuple-element.22), channel_id=1, source_target_pairs={{0,4},{4,8},{8,12},{1,5},{5,9},{9,13},{2,6},{6,10},{10,14},{3,7},{... | collective-permute-start | bytes 786440 | tf_op jit(solution)/shard_map/ppermute | solution.py:15
  37.9 14.0 %collective-permute-start.5 = (bf16[128,1,16,64]{3,2,1,0:T(8,128)(2,1)}, bf16[128,1,16,64]{3,2,1,0:T(8,128)(2,1)S(1)}, u32[]{:S(2)}, u32[]{:S(2)}) collective-permute-start(bf16[128,1,16,64]{3,2,1,0:T(8,128)(2,1)} %get-tuple-element.21), channel_id=1, source_target_pairs={{4,0},{8,4},{12,8},{5,1},{9,5},{13,9},{6,2},{10,6},{14,10},{7,3},{... | collective-permute-start | bytes 786440 | tf_op jit(solution)/shard_map/ppermute | solution.py:17
  43.8 5.9 %copy-start.4 = (bf16[32,6,32,128]{3,2,1,0:T(8,128)(2,1)}, bf16[32,6,32,128]{3,2,1,0:T(8,128)(2,1)S(1)}, u32[]{:S(2)}) copy-start(bf16[32,6,32,128]{3,2,1,0:T(8,128)(2,1)S(1)} %constant_dynamic-update-slice_fusion) | copy-start | bytes 4718596
  44.0 29.2 %collective-permute-start.3 = (bf16[32,6,1,128]{3,0,2,1:T(8,128)(2,1)S(1)}, bf16[32,6,1,128]{3,0,2,1:T(8,128)(2,1)S(1)}, u32[]{:S(2)}, u32[]{:S(2)}) collective-permute-start(bf16[32,6,1,128]{3,0,2,1:T(8,128)(2,1)S(1)} %copy.106), channel_id=1, source_target_pairs={{1,0},{3,2},{5,4},{7,6},{9,8},{11,10},{13,12},{15,14},{17,16},{19,... | collective-permute-start | bytes 147464 | tf_op jit(solution)/shard_map/ppermute | solution.py:17
  45.3 37.6 %collective-permute-start.2 = (bf16[32,6,1,128]{3,0,2,1:T(8,128)(2,1)S(1)}, bf16[32,6,1,128]{3,0,2,1:T(8,128)(2,1)S(1)}, u32[]{:S(2)}, u32[]{:S(2)}) collective-permute-start(bf16[32,6,1,128]{3,0,2,1:T(8,128)(2,1)S(1)} %copy.105), channel_id=1, source_target_pairs={{0,1},{2,3},{4,5},{6,7},{8,9},{10,11},{12,13},{14,15},{16,17},{18,... | collective-permute-start | bytes 147464 | tf_op jit(solution)/shard_map/ppermute | solution.py:15
  52.0 1.4 copy-start.1
  54.6 10.0 %copy-start.2 = (bf16[128,4,16,64]{3,2,1,0:T(8,128)(2,1)S(1)}, bf16[128,4,16,64]{3,2,1,0:T(8,128)(2,1)}, u32[]{:S(2)}) copy-start(bf16[128,4,16,64]{3,2,1,0:T(8,128)(2,1)} %copy-done.1) | copy-start | bytes 3145732
  67.5 170.7 %collective-permute-start.7 = (bf16[128,4,1,64]{3,2,1,0:T(2,128)(2,1)}, bf16[128,4,1,64]{3,2,1,0:T(2,128)(2,1)}, u32[]{:S(2)}, u32[]{:S(2)}) collective-permute-start(bf16[128,4,1,64]{3,2,1,0:T(2,128)(2,1)} %get-tuple-element.18), channel_id=1, source_target_pairs={{1,0},{3,2},{5,4},{7,6},{9,8},{11,10},{13,12},{15,14},{17,16},{19,... | collective-permute-start | bytes 196616 | tf_op jit(solution)/shard_map/ppermute | solution.py:17
  68.8 170.5 %collective-permute-start.6 = (bf16[128,4,1,64]{3,2,1,0:T(2,128)(2,1)}, bf16[128,4,1,64]{3,2,1,0:T(2,128)(2,1)}, u32[]{:S(2)}, u32[]{:S(2)}) collective-permute-start(bf16[128,4,1,64]{3,2,1,0:T(2,128)(2,1)} %get-tuple-element.17), channel_id=1, source_target_pairs={{0,1},{2,3},{4,5},{6,7},{8,9},{10,11},{12,13},{14,15},{16,17},{18,... | collective-permute-start | bytes 196616 | tf_op jit(solution)/shard_map/ppermute | solution.py:15
  109.3 14.3 %copy-start.10 = (pred[8,9]{0,1:T(8,128)(4,1)S(1)}, pred[8,9]{0,1:T(8,128)(4,1)}, u32[]{:S(2)}) copy-start(pred[8,9]{0,1:T(8,128)(4,1)} %constant.10) | copy-start | bytes 220
  160.6 28.7 %copy-start.7 = (bf16[1,128,2,16,64]{1,0,4,3,2:T(2,128)(2,1)S(1)}, bf16[1,128,2,16,64]{1,0,4,3,2:T(2,128)(2,1)}, u32[]{:S(2)}) copy-start(bf16[1,128,2,16,64]{1,0,4,3,2:T(2,128)(2,1)} %copy.98) | copy-start | bytes 1572868
  234.3 3.0 %copy-start.6 = (bf16[128,2,1024]{2,1,0:T(2,128)(2,1)S(1)}, bf16[128,2,1024]{2,1,0:T(2,128)(2,1)}, u32[]{:S(2)}) copy-start(bf16[128,2,1024]{2,1,0:T(2,128)(2,1)} %all-reduce.2) | copy-start | bytes 1572868
  234.3 6.0 %copy-start.3 = (bf16[128,4,16,64]{0,3,2,1:T(8,128)(2,1)S(1)}, bf16[128,4,16,64]{0,3,2,1:T(8,128)(2,1)}, u32[]{:S(2)}) copy-start(bf16[128,4,16,64]{0,3,2,1:T(8,128)(2,1)} %copy.88) | copy-start | bytes 3145732
  241.6 0.8 copy-start.9
Sparse Core Ops, SparseCore 0:
  237.4 34.1 reduce-scatter.1
where the time goes:
time: 280 us; the launch traced here: 278 us
  local copies, waits for them, and re-layouts  113 us (40%)
  matrix products  63.7 us (23%)
  blocking collectives  41.7 us (15%)
  starting transfers between devices  23.4 us (8%)
  between operations  15 us (5%)
  other arithmetic  12.6 us (4%)
  waiting for transfers between devices  9.55 us (3%)
    transpose x1, matrix products, body(): filter_term.transpose(1, 0, 2, 3, 4).reshape(n_out, local_in, 64)  45 us
    broadcast_in_dim x2, local copies, waits for them, and re-layouts, strided(): padded[None]  33 us
    unnamed x1, blocking collectives  27.5 us
    ppermute x4, starting transfers between devices, padded_2(): lax.ppermute(tail, axis, [(i, (i + 1) % count) for i in range(ends)])  18.1 us
    conv_general_dilated x5, local copies, waits for them, and re-layouts, strided(): lax.conv_general_dilated(padded[None], filters, (2, 2, 2), ((0, 0), (0, 0...  14.9 us
    all_gather x1, blocking collectives, body(): gathered = lax.all_gather(local_grad, 'ch', axis=0, tiled=True)  14.2 us
    concatenate x4, local copies, waits for them, and re-layouts, padded_2(): jnp.concatenate([lax.ppermute(tail, axis, [(i, (i + 1) % count) for i in...  13.1 us
    unnamed x31, local copies, waits for them, and re-layouts  13 us
  transfers between devices with their start and end apart: 9, of which 2 were waited for; matrix products, arithmetic and copies ran while one was open for 67% of the time, Pallas kernels for 0%

commit v1 on v0

v1 whole, which is shorter than its diff:
```python
import functools

import jax
import jax.numpy as jnp
from jax import lax
from jax.experimental import pallas as pl
from jax.experimental.pallas import tpu as pltpu
from jax.sharding import PartitionSpec as P

MESH = pl.DeviceIdType.MESH
F32 = jnp.float32
BF16 = jnp.bfloat16


def kernel_body(
    nz, nx, vol, wts, cot, feat, vgrad, kgrad,
    halo, split, edge_out, edge_in, cols, gbuf, fsum, fsend, frecv, kpart, krecv, ksend, kzin, wide, rows32, wt_t,
    v_send, v_recv, g_send, g_recv, gz_send, gz_recv, e_send, e_recv, ge_sem, f_send, f_recv, ks_sem, kz_send, kz_recv, own_sem,
):
    z = lax.axis_index("sp")
    x = lax.axis_index("ch")
    s = lax.axis_index("sub")
    other = 1 - s
    cin = vol.shape[0]
    high = vol.shape[2]
    n_out = wts.shape[0]
    local_out = cot.shape[1]
    area = cot.shape[2]
    tiles = area // 128
    taps = 16 * cin
    has_low = z > 0
    has_high = z < nz - 1

    for side in (0, 128 + area):
        gbuf[:, :, side : side + 128] = jnp.zeros((4, n_out, 128), BF16)

    @pl.when(jnp.logical_not(has_low))
    def _():
        halo[0] = jnp.zeros(halo.shape[1:], BF16)
        gbuf[0] = jnp.zeros(gbuf.shape[1:], BF16)

    @pl.when(jnp.logical_not(has_high))
    def _():
        halo[1] = jnp.zeros(halo.shape[1:], BF16)
        gbuf[3] = jnp.zeros(gbuf.shape[1:], BF16)

    barrier = pltpu.get_barrier_semaphore()
    for k in range(1, nz):
        pl.semaphore_signal(barrier, 1, device_id={"sp": lax.rem(z + k, nz)}, device_id_type=MESH)
    for k in range(1, nx):
        pl.semaphore_signal(barrier, 1, device_id={"ch": lax.rem(x + k, nx)}, device_id_type=MESH)
    pl.semaphore_signal(barrier, 1, device_id={"sub": other}, device_id_type=MESH)
    pl.semaphore_wait(barrier, nz + nx - 1)

    def remote(src, dst, send, recv, target):
        return pltpu.make_async_remote_copy(
            src_ref=src, dst_ref=dst, send_sem=send, recv_sem=recv, device_id=target, device_id_type=MESH
        )

    low = jnp.maximum(z - 1, 0)
    up = jnp.minimum(z + 1, nz - 1)
    v_down = remote(vol.at[:, 0], halo.at[1], v_send.at[0], v_recv.at[1], {"sp": low})
    v_up = remote(vol.at[:, 3], halo.at[0], v_send.at[1], v_recv.at[0], {"sp": up})
    pl.when(has_low)(v_down.start)
    pl.when(has_high)(v_up.start)

    def g_rows(owner):
        return gbuf.at[pl.ds(1, 2), pl.ds(pl.multiple_of(owner * local_out, local_out), local_out), pl.ds(128, area)]

    g_copies = []
    for k in range(1, nx):
        g_copies.append(remote(cot, g_rows(x), g_send.at[k - 1], g_recv.at[k - 1], {"ch": lax.rem(x + k, nx)}))
        g_copies[-1].start()
    own = pltpu.make_async_copy(cot, g_rows(x), own_sem)
    own.start()

    k_at = lax.broadcasted_iota(jnp.int32, (128, 128), 0)
    l_at = lax.broadcasted_iota(jnp.int32, (128, 128), 1)
    pick = [
        (k_at == 2 * (l_at % 64) + (l_at // 64 + 2 * half) - 1).astype(BF16) for half in range(2)
    ]
    first = lax.broadcasted_iota(jnp.int32, (cin, 128), 1) < 64

    def splits(plane, cells):
        flat = cells.reshape(cin * high, 128)
        for half in range(2):
            split[plane, half] = jnp.dot(flat, pick[half], preferred_element_type=F32)
            rim = jnp.where(
                s == 0,
                split.at[plane, half][pl.ds(high - 1, cin, stride=high), :],
                split.at[plane, half][pl.ds(0, cin, stride=high), :],
            )
            edge_out[plane, half] = rim.astype(BF16)

    def own_split(i, _):
        splits(i + 1, vol[:, i])
        return 0

    lax.fori_loop(0, 4, own_split, 0)

    def edge_copy(index, start, count):
        return remote(
            edge_out.at[pl.ds(start, count)], edge_in.at[pl.ds(start, count)],
            e_send.at[index], e_recv.at[index], {"sub": other},
        )

    e_own = edge_copy(0, 1, 4)
    e_own.start()

    own.wait()
    for k in range(1, nx):
        g_copies[k - 1].wait_send()
        origin = lax.rem(x + nx - k, nx)
        remote(cot, g_rows(origin), g_send.at[k - 1], g_recv.at[k - 1], {"ch": origin}).wait_recv()

    def g_plane(at):
        return gbuf.at[at, :, pl.ds(128, area)]

    g_down = remote(g_plane(1), g_plane(3), gz_send.at[0], gz_recv.at[1], {"sp": low})
    g_up = remote(g_plane(2), g_plane(0), gz_send.at[1], gz_recv.at[0], {"sp": up})
    pl.when(has_low)(g_down.start)
    pl.when(has_high)(g_up.start)

    def build(plane):
        for half in range(2):
            rim = edge_in[plane, half].astype(F32)
            above = jnp.where(s == 1, rim, 0.0)
            below = jnp.where(s == 0, rim, 0.0)

            def row(j):
                if j < 0:
                    return above
                if j >= high:
                    return below
                return split.at[plane, half][pl.ds(j, cin, stride=high), :]

            for b in range(4):
                for t in range(tiles):
                    a_row, b_row = row(4 * t + b - 1), row(4 * t + b + 1)
                    left = jnp.where(first, a_row, pltpu.roll(b_row, 64, 1))
                    right = jnp.where(first, pltpu.roll(a_row, 64, 1), b_row)
                    cols[plane, b, 2 * half, :, t * 128 : t * 128 + 128] = left.astype(BF16)
                    cols[plane, b, 2 * half + 1, :, t * 128 : t * 128 + 128] = right.astype(BF16)

    def build_own(i, _):
        build(i + 1)
        return 0

    e_own.wait()
    lax.fori_loop(0, 4, build_own, 0)

    @pl.when(has_low)
    def _():
        v_down.wait_send()
        v_up.wait_recv()

    @pl.when(has_high)
    def _():
        v_up.wait_send()
        v_down.wait_recv()

    def halo_split(i, _):
        splits(5 * i, halo[i])
        return 0

    lax.fori_loop(0, 2, halo_split, 0)
    e_low, e_high = edge_copy(1, 0, 1), edge_copy(2, 5, 1)
    e_low.start()
    e_high.start()

    for odd in range(2):
        for place in range(2):
            a = (3, 1, 2, 0)[2 * odd + place]
            block = wts[:, a * taps : (a + 1) * taps].astype(F32)
            wt_t[odd, :, place * n_out : (place + 1) * n_out] = block.T.astype(BF16)

    e_low.wait()
    e_high.wait()

    def build_halo(i, _):
        build(5 * i)
        return 0

    lax.fori_loop(0, 2, build_halo, 0)

    def forward(step, _):
        d, at = step // (area // 256), step % (area // 256)
        lanes = pl.ds(pl.multiple_of(at * 256, 256), 256)
        block = cols[pl.ds(2 * d, 4), :, :, :, lanes].reshape(4 * taps, 256)
        part = jnp.dot(wts[...], block, preferred_element_type=F32)
        fsum[d, :, lanes] = part
        fsend[d, :, lanes] = part.astype(BF16)
        return 0

    lax.fori_loop(0, 2 * (area // 256), forward, 0)

    def out_rows(ref, owner):
        return ref.at[:, pl.ds(pl.multiple_of(owner * local_out, local_out), local_out), :]

    f_copies = []
    for k in range(1, nx):
        peer = lax.rem(x + k, nx)
        f_copies.append(remote(out_rows(fsend, peer), frecv.at[k - 1], f_send.at[k - 1], f_recv.at[k - 1], {"ch": peer}))
        f_copies[-1].start()

    rows = n_out // (2 * nz)

    def kernel_part(a, _):
        total = 0.0
        for d in range(2):
            total += lax.dot_general(
                gbuf[1 + d, :, 128 : 128 + area],
                cols[2 * d + a].reshape(taps, area),
                (((1,), (1,)), ((), ())),
                preferred_element_type=F32,
            )
        for block in range(2 * nz):
            kpart[block // 2, block % 2, :, pl.ds(pl.multiple_of(a * taps, 128), taps)] = total[block * rows : (block + 1) * rows]
        return 0

    lax.fori_loop(0, 4, kernel_part, 0)
    k_pair = remote(kpart.at[:, other], krecv, ks_sem.at[0], ks_sem.at[1], {"sub": other})
    k_pair.start()

    @pl.when(has_low)
    def _():
        g_down.wait_send()
        g_up.wait_recv()

    @pl.when(has_high)
    def _():
        g_up.wait_send()
        g_down.wait_recv()

    g_edge = remote(
        gbuf.at[:, :, pl.ds(pl.multiple_of(jnp.where(s == 0, area, 128), 128), 128)],
        gbuf.at[:, :, pl.ds(pl.multiple_of(jnp.where(s == 0, 0, 128 + area), 128), 128)],
        ge_sem.at[0], ge_sem.at[1], {"sub": other},
    )
    g_edge.start()

    k_pair.wait_send()
    remote(kpart.at[:, other], krecv, ks_sem.at[0], ks_sem.at[1], {"sub": other}).wait_recv()
    for block in range(nz):
        mine = jnp.where(s == 0, kpart[block, 0], kpart[block, 1]) + krecv[block]
        krecv[block] = mine
        ksend[block, 0:rows, :] = mine.astype(BF16)
    k_copies = []
    for k in range(1, nz):
        peer = lax.rem(z + k, nz)
        k_copies.append(remote(ksend.at[peer], kzin.at[k - 1], kz_send.at[k - 1], kz_recv.at[k - 1], {"sp": peer}))
        k_copies[-1].start()

    g_edge.wait_send()
    remote(
        gbuf.at[:, :, pl.ds(0, 128)],
        gbuf.at[:, :, pl.ds(pl.multiple_of(jnp.where(s == 0, 128 + area, 0), 128), 128)],
        ge_sem.at[0], ge_sem.at[1], {"sub": other},
    ).wait_recv()

    lane = lax.broadcasted_iota(jnp.int32, (cin, 128), 1) % 64
    inner_low, inner_high = lane > 0, lane < 63
    weave = (l_at == 2 * (k_at % 64) + k_at // 64).astype(BF16)

    def volume_plane(i, _):
        block = gbuf[pl.ds((i + 1) // 2, 2)].reshape(2 * n_out, 256 + area)
        wide[...] = jnp.dot(wt_t[i % 2], block, preferred_element_type=F32)

        def term(b, r, t):
            lanes = slice(t * 128, t * 128 + 128)

            def tap(e):
                return wide[(4 * b + e) * cin : (4 * b + e + 1) * cin, lanes]

            if r == 0:
                return tap(1) + jnp.where(inner_low, pltpu.roll(tap(3), 1, 1), 0.0)
            return tap(2) + jnp.where(inner_high, pltpu.roll(tap(0), 127, 1), 0.0)

        for q in range(2):
            kept = [None, None]
            for t in range(1, tiles + 1):
                both = []
                for r in range(2):
                    if q == 0:
                        before = pltpu.roll(term(3, r, t - 1), 64, 1) if kept[r] is None else kept[r]
                        after = pltpu.roll(term(3, r, t), 64, 1)
                        base = term(1, r, t)
                    else:
                        before = pltpu.roll(term(0, r, t), 64, 1) if kept[r] is None else kept[r]
                        after = pltpu.roll(term(0, r, t + 1), 64, 1)
                        base = term(2, r, t)
                    kept[r] = after
                    both.append(base + jnp.where(first, before, after))
                n = 2 * (t - 1)
                rows32[pl.ds(2 * n + q, cin, stride=high), :] = jnp.where(first, both[0], pltpu.roll(both[1], 64, 1))
                rows32[pl.ds(2 * n + 2 + q, cin, stride=high), :] = jnp.where(first, pltpu.roll(both[0], 64, 1), both[1])
        woven = jnp.dot(rows32[...].astype(BF16), weave, preferred_element_type=F32)
        vgrad[:, i] = woven.astype(BF16).reshape(cin, high, 128)
        return 0

    lax.fori_loop(0, 4, volume_plane, 0)

    for d in range(2):
        total = fsum[d, pl.ds(pl.multiple_of(x * local_out, local_out), local_out), :]
        for k in range(1, nx):
            if d == 0:
                f_copies[k - 1].wait()
            total = total + frecv[k - 1, d].astype(F32)
        feat[d] = total.astype(BF16)

    result = krecv[z]
    for k in range(1, nz):
        k_copies[k - 1].wait()
        result = result + kzin[k - 1, 0:rows, :].astype(F32)
    kgrad[...] = result


def body(volume, kernel, cotangent):
    n_out, cin = kernel.shape[:2]
    nz, nx = lax.axis_size("sp"), lax.axis_size("ch")
    local_out, depth, area = cotangent.shape
    high = volume.shape[2]
    rows = n_out // (2 * nz)
    padded_rows = -(-rows // 16) * 16
    weights = kernel.transpose(0, 2, 1).reshape(n_out, 64 * cin)
    grads = cotangent.transpose(1, 0, 2)
    vmem = pl.BlockSpec(memory_space=pltpu.VMEM)
    dma = pltpu.SemaphoreType.DMA
    feat, vgrad, kgrad = pl.pallas_call(
        functools.partial(kernel_body, nz, nx),
        out_shape=(
            jax.ShapeDtypeStruct((depth, local_out, area), BF16),
            jax.ShapeDtypeStruct(volume.shape, BF16),
            jax.ShapeDtypeStruct((rows, 64 * cin), F32),
        ),
        in_specs=[vmem] * 3,
        out_specs=[vmem] * 3,
        scratch_shapes=[
            pltpu.VMEM((2, cin, high, 128), BF16),
            pltpu.VMEM((6, 2, cin * high, 128), F32),
            pltpu.VMEM((6, 2, cin, 128), BF16),
            pltpu.VMEM((6, 2, cin, 128), BF16),
            pltpu.VMEM((6, 4, 4, cin, area), BF16),
            pltpu.VMEM((4, n_out, 256 + area), BF16),
            pltpu.VMEM((depth, n_out, area), F32),
            pltpu.VMEM((depth, n_out, area), BF16),
            pltpu.VMEM((nx - 1, depth, local_out, area), BF16),
            pltpu.VMEM((nz, 2, rows, 64 * cin), F32),
            pltpu.VMEM((nz, rows, 64 * cin), F32),
            pltpu.VMEM((nz, padded_rows, 64 * cin), BF16),
            pltpu.VMEM((nz - 1, padded_rows, 64 * cin), BF16),
            pltpu.VMEM((16 * cin, 256 + area), F32),
            pltpu.VMEM((cin * high, 128), F32),
            pltpu.VMEM((2, 16 * cin, 2 * n_out), BF16),
            dma((2,)), dma((2,)),
            dma((nx - 1,)), dma((nx - 1,)),
            dma((2,)), dma((2,)),
            dma((3,)), dma((3,)),
            dma((2,)),
            dma((nx - 1,)), dma((nx - 1,)),
            dma((2,)),
            dma((nz - 1,)), dma((nz - 1,)),
            dma,
        ],
        compiler_params=pltpu.CompilerParams(
            collective_id=0, has_side_effects=True, vmem_limit_bytes=56 * 1024 * 1024
        ),
    )(volume, weights, grads)
    features = feat.transpose(1, 0, 2)
    kernel_grad = kgrad.reshape(rows, 64, cin).transpose(0, 2, 1)
    return (features, vgrad, kernel_grad)


def solution(mesh):
    return jax.shard_map(
        body,
        mesh=mesh,
        in_specs=(
            P("ch", ("grp", "sp"), "sub", None),
            P(None, "ch", None),
            P("ch", ("grp", "sp"), "sub"),
        ),
        out_specs=(
            P("ch", ("grp", "sp"), "sub"),
            P("ch", ("grp", "sp"), "sub", None),
            P(("grp", "sp", "sub"), "ch", None),
        ),
        check_vma=False,
    )
```

time: 280 us -> 48.1 us (0.17)
  local copies, waits for them, and re-layouts: 113 us -> 7.21 us
  matrix products: 63.7 us -> 0 us
  blocking collectives: 41.7 us -> 0 us
  Pallas kernels: 0 us -> 40 us
  starting transfers between devices: 23.4 us -> 0 us
  between operations: 15 us -> 0.68 us
  other arithmetic: 12.6 us -> 0 us
  waiting for transfers between devices: 9.55 us -> 0 us
    transpose x1 -> x0, matrix products: 45 us -> none  [body(): filter_term.transpose(1, 0, 2, 3, 4).reshape(n_out, local_in, 64)]
    pallas_call x0 -> x1, Pallas kernels: none -> 40 us  [body(): pl.pallas_call(functools.partial(kernel_body, nz, nx), out_shape=(jax.Sha...]
    broadcast_in_dim x4 -> x0, local copies, waits for them, and re-layouts: 35.7 us -> none  [the longest x2 33 us: strided(): padded[None]]
    unnamed x1 -> x0, blocking collectives: 27.5 us -> none
    ppermute x8 -> x0, starting transfers between devices: 23.4 us -> none  [the longest x4 18.1 us: padded_2(): lax.ppermute(tail, axis, [(i, (i + 1) % count) for i in range(ends)])]
    ppermute x4 -> x0, local copies, waits for them, and re-layouts: 21.5 us -> none  [the longest x2 10.8 us: padded_2(): lax.ppermute(tail, axis, [(i, (i + 1) % count) for i in range(ends)])]
    conv_general_dilated x2 -> x0, matrix products: 18.7 us -> none  [the longest x1 10.4 us: body(): lax.conv_general_dilated(grad_rims[None], flipped, (1, 1, 1), ((0, 0), (0...]
    conv_general_dilated x7 -> x0, local copies, waits for them, and re-layouts: 15.1 us -> none  [the longest x5 14.9 us: strided(): lax.conv_general_dilated(padded[None], filters, (2, 2, 2), ((0, 0), (0, 0...]
  transfers between devices with their start and end apart: 9 -> 0, of which waited for: 2 -> 0; matrix products, arithmetic and copies ran while one was open for 67% -> 0% of each run, Pallas kernels for 0% -> 0%
where the time goes in v1:
time: 48.1 us; the launch traced here: 47.9 us
  Pallas kernels  40 us (83%)
  local copies, waits for them, and re-layouts  7.21 us (15%)
  between operations  0.68 us (1%)
    pallas_call x1, Pallas kernels, body(): pl.pallas_call(functools.partial(kernel_body, nz, nx), out_shape=(jax.Sha...  40 us
    unnamed x11, local copies, waits for them, and re-layouts  5.04 us
    reshape x1, local copies, waits for them, and re-layouts, body(): kernel_grad = kgrad.reshape(rows, 64, cin).transpose(0, 2, 1)  1.16 us
    reshape x1, local copies, waits for them, and re-layouts, body(): weights = kernel.transpose(0, 2, 1).reshape(n_out, 64 * cin)  1.01 us

profile of v1, /device:TPU:0, one launch (start us, length us, event | category | flops | bytes accessed | tf_op | source)
XLA Modules:
  0.0 47.9 jit_solution(9192436195537587176)
XLA Ops:
  0.6 1.4 %copy.10 = bf16[128,32,64]{0,1,2:T(8,128)(2,1)S(1)} copy(bf16[128,32,64]{0,2,1:T(8,128)(2,1)} %param.4) | data formatting | bytes 1048576 | tf_op args[1]
  2.0 0.0 copy-start.1
  2.0 1.0 %copy.12.wts = bf16[128,2048]{1,0:T(8,128)(2,1)} copy(bf16[128,2048]{0,1:T(8,128)(2,1)S(1)} %bitcast.9) | data formatting | bytes 1048576 | tf_op jit(solution)/shard_map/reshape | solution.py:325
  3.0 0.0 copy-done.1
  3.0 0.8 %copy.16 = bf16[64,2,1024]{2,0,1:T(8,128)(2,1)} copy(bf16[64,2,1024]{2,1,0:T(2,128)(2,1)S(1)} %copy-done.1) | data formatting | bytes 524288 | tf_op args[2]
  3.8 40.0 %shard_map.58 = (bf16[2,64,1024]{2,1,0:T(8,128)(2,1)}, bf16[32,4,32,128]{3,2,1,0:T(8,128)(2,1)}, f32[16,2048]{1,0:T(8,128)}) custom-call(bf16[32,4,32,128]{3,2,1,0:T(8,128)(2,1)} %vol.1, bf16[128,2048]{1,0:T(8,128)(2,1)} %copy.12.wts, bf16[2,64,1024]{2,1,0:T(8,128)(2,1)} %bitcast.10), custom_call_target="tpu_custom_call" | custom-call | tf_op jit(solution)/shard_map/pallas_call | solution.py:329
  43.8 0.0 copy-start
  43.8 1.2 %reshape.13 = f32[16,64,32]{2,1,0:T(8,128)S(1)} reshape(f32[16,2048]{1,0:T(8,128)} %get-tuple-element.8) | data formatting | bytes 262144 | tf_op jit(solution)/shard_map/reshape | solution.py:370
  45.0 0.0 copy-start.2
  45.0 0.9 %copy.14 = f32[16,32,64]{2,1,0:T(8,128)} copy(f32[16,32,64]{1,2,0:T(8,128)S(1)} %bitcast.8) | data formatting | bytes 262144
  45.9 0.0 copy-done.2
  45.9 1.0 %copy.13 = bf16[64,2,1024]{2,1,0:T(2,128)(2,1)} copy(bf16[64,2,1024]{2,0,1:T(8,128)(2,1)S(1)} %bitcast.11) | data formatting | bytes 524288
  46.9 0.0 copy-done
  46.9 1.0 %copy.18 = bf16[32,4,32,128]{3,2,1,0:T(8,128)(2,1)} copy(bf16[32,4,32,128]{3,2,1,0:T(8,128)(2,1)S(1)} %copy-done) | data formatting | bytes 2097152
Async XLA Ops:
  2.0 1.0 %copy-start.1 = (bf16[64,2,1024]{2,1,0:T(2,128)(2,1)S(1)}, bf16[64,2,1024]{2,1,0:T(2,128)(2,1)}, u32[]{:S(2)}) copy-start(bf16[64,2,1024]{2,1,0:T(2,128)(2,1)} %param.5) | copy-start | bytes 786436
  43.8 3.1 %copy-start = (bf16[32,4,32,128]{3,2,1,0:T(8,128)(2,1)S(1)}, bf16[32,4,32,128]{3,2,1,0:T(8,128)(2,1)}, u32[]{:S(2)}) copy-start(bf16[32,4,32,128]{3,2,1,0:T(8,128)(2,1)} %get-tuple-element.19) | copy-start | bytes 3145732
  45.0 1.0 %copy-start.2 = (bf16[2,64,1024]{2,1,0:T(8,128)(2,1)S(1)}, bf16[2,64,1024]{2,1,0:T(8,128)(2,1)}, u32[]{:S(2)}) copy-start(bf16[2,64,1024]{2,1,0:T(8,128)(2,1)} %get-tuple-element.6) | copy-start | bytes 786436

commit v2 on v1

v2 whole, which is shorter than its diff:
```python
import functools

import jax
import jax.numpy as jnp
from jax import lax
from jax.experimental import pallas as pl
from jax.experimental.pallas import tpu as pltpu
from jax.sharding import PartitionSpec as P

MESH = pl.DeviceIdType.MESH
F32 = jnp.float32
BF16 = jnp.bfloat16


def kernel_body(
    nz, nx, vol, wts, cot, feat, vgrad, kgrad,
    halo, split, edge_out, edge_in, cols, gbuf, fsum, fsend, frecv, kpart, krecv, ksend, kzin, wide, rows32, wt_t,
    v_send, v_recv, g_send, g_recv, gz_send, gz_recv, e_send, e_recv, ge_sem, f_send, f_recv, ks_sem, kz_send, kz_recv, own_sem,
):
    z = lax.axis_index("sp")
    x = lax.axis_index("ch")
    s = lax.axis_index("sub")
    other = 1 - s
    cin = vol.shape[0]
    high = vol.shape[2]
    n_out = wts.shape[0]
    local_out = cot.shape[1]
    area = cot.shape[2]
    tiles = area // 128
    taps = 16 * cin
    pitch = high + 8
    has_low = z > 0
    has_high = z < nz - 1

    for side in (0, 128 + area):
        gbuf[:, :, side : side + 128] = jnp.zeros((4, n_out, 128), BF16)

    @pl.when(jnp.logical_not(has_low))
    def _():
        halo[0] = jnp.zeros(halo.shape[1:], BF16)
        gbuf[0] = jnp.zeros(gbuf.shape[1:], BF16)

    @pl.when(jnp.logical_not(has_high))
    def _():
        halo[1] = jnp.zeros(halo.shape[1:], BF16)
        gbuf[3] = jnp.zeros(gbuf.shape[1:], BF16)

    barrier = pltpu.get_barrier_semaphore()
    for k in range(1, nz):
        pl.semaphore_signal(barrier, 1, device_id={"sp": lax.rem(z + k, nz)}, device_id_type=MESH)
    for k in range(1, nx):
        pl.semaphore_signal(barrier, 1, device_id={"ch": lax.rem(x + k, nx)}, device_id_type=MESH)
    pl.semaphore_signal(barrier, 1, device_id={"sub": other}, device_id_type=MESH)

    k_at = lax.broadcasted_iota(jnp.int32, (128, 128), 0)
    l_at = lax.broadcasted_iota(jnp.int32, (128, 128), 1)
    pick = [
        (k_at == 2 * (l_at % 64) + (l_at // 64 + 2 * half) - 1).astype(BF16) for half in range(2)
    ]
    first = lax.broadcasted_iota(jnp.int32, (cin, 128), 1) < 64

    def splits(plane, cells):
        flat = cells.reshape(cin * high, 128)
        for half in range(2):
            value = jnp.dot(flat, pick[half], preferred_element_type=F32)
            for c in range(cin):
                split[plane, half, c * pitch : c * pitch + high, :] = value[c * high : (c + 1) * high]
            rim = jnp.where(
                s == 0,
                split.at[plane, half][pl.ds(high - 1, cin, stride=pitch), :],
                split.at[plane, half][pl.ds(0, cin, stride=pitch), :],
            )
            edge_out[plane, half] = rim.astype(BF16)

    def own_split(i, _):
        splits(i + 1, vol[:, i])
        return 0

    lax.fori_loop(0, 4, own_split, 0)

    pl.semaphore_wait(barrier, nz + nx - 1)

    def remote(src, dst, send, recv, target):
        return pltpu.make_async_remote_copy(
            src_ref=src, dst_ref=dst, send_sem=send, recv_sem=recv, device_id=target, device_id_type=MESH
        )

    low = jnp.maximum(z - 1, 0)
    up = jnp.minimum(z + 1, nz - 1)
    v_down = remote(vol.at[:, 0], halo.at[1], v_send.at[0], v_recv.at[1], {"sp": low})
    v_up = remote(vol.at[:, 3], halo.at[0], v_send.at[1], v_recv.at[0], {"sp": up})
    pl.when(has_low)(v_down.start)
    pl.when(has_high)(v_up.start)

    def g_rows(owner):
        return gbuf.at[pl.ds(1, 2), pl.ds(pl.multiple_of(owner * local_out, local_out), local_out), pl.ds(128, area)]

    g_copies = []
    for k in range(1, nx):
        g_copies.append(remote(cot, g_rows(x), g_send.at[k - 1], g_recv.at[k - 1], {"ch": lax.rem(x + k, nx)}))
        g_copies[-1].start()
    own = pltpu.make_async_copy(cot, g_rows(x), own_sem)
    own.start()

    def edge_copy(index, start, count):
        return remote(
            edge_out.at[pl.ds(start, count)], edge_in.at[pl.ds(start, count)],
            e_send.at[index], e_recv.at[index], {"sub": other},
        )

    e_own = edge_copy(0, 1, 4)
    e_own.start()

    def build(plane):
        for half in range(2):
            rim = edge_in[plane, half].astype(F32)
            above = jnp.where(s == 1, rim, 0.0)
            below = jnp.where(s == 0, rim, 0.0)

            def row(j):
                if j < 0:
                    return above
                if j >= high:
                    return below
                return split.at[plane, half][pl.ds(j, cin, stride=pitch), :]

            for start in (-1, 0):
                a_row = row(start)
                a_turned = pltpu.roll(a_row, 64, 1)
                for j in range(start, high - 1, 2):
                    b_row = row(j + 2)
                    b_turned = pltpu.roll(b_row, 64, 1)
                    b, t = (j + 1) % 4, (j + 1) // 4
                    lanes = slice(t * 128, t * 128 + 128)
                    cols[plane, b, 2 * half, :, lanes] = jnp.where(first, a_row, b_turned).astype(BF16)
                    cols[plane, b, 2 * half + 1, :, lanes] = jnp.where(first, a_turned, b_row).astype(BF16)
                    a_row, a_turned = b_row, b_turned

    def g_plane(at):
        return gbuf.at[at, :, pl.ds(128, area)]

    g_down = remote(g_plane(1), g_plane(3), gz_send.at[0], gz_recv.at[1], {"sp": low})
    g_up = remote(g_plane(2), g_plane(0), gz_send.at[1], gz_recv.at[0], {"sp": up})
    def spread():
        own.wait()
        for k in range(1, nx):
            g_copies[k - 1].wait_send()
            origin = lax.rem(x + nx - k, nx)
            remote(cot, g_rows(origin), g_send.at[k - 1], g_recv.at[k - 1], {"ch": origin}).wait_recv()
        pl.when(has_low)(g_down.start)
        pl.when(has_high)(g_up.start)

    def build_own(i, _):
        pl.when(i == 2)(spread)
        build(i + 1)
        return 0

    e_own.wait()
    lax.fori_loop(0, 4, build_own, 0)

    rows = n_out // (2 * nz)

    def kernel_part(group, index, a):
        total = 0.0
        for d in range(2):
            total += lax.dot_general(
                gbuf[1 + d, :, 128 : 128 + area],
                cols[2 * d + a].reshape(taps, area),
                (((1,), (1,)), ((), ())),
                preferred_element_type=F32,
            )
        lanes = pl.ds(pl.multiple_of(index * taps, 128), taps)
        for block in range(2 * nz):
            kpart[group, block // 2, block % 2, :, lanes] = total[block * rows : (block + 1) * rows]

    def k_pair(group):
        return remote(
            kpart.at[group, :, other], krecv.at[group], ks_sem.at[0, group], ks_sem.at[1, group], {"sub": other}
        )

    def k_copy(group, k):
        peer = lax.rem(z + k, nz)
        return remote(
            ksend.at[group, peer], kzin.at[group, k - 1],
            kz_send.at[group, k - 1], kz_recv.at[group, k - 1], {"sp": peer},
        )

    def k_reduce(group):
        k_pair(group).wait()
        for block in range(nz):
            mine = jnp.where(s == 0, kpart[group, block, 0], kpart[group, block, 1]) + krecv[group, block]
            krecv[group, block] = mine
            ksend[group, block, 0:rows, :] = mine.astype(BF16)
        for k in range(1, nz):
            k_copy(group, k).start()

    def inner_parts(index, _):
        kernel_part(0, index, 1 + index)
        return 0

    lax.fori_loop(0, 2, inner_parts, 0)
    k_pair(0).start()

    @pl.when(has_low)
    def _():
        v_down.wait_send()
        v_up.wait_recv()

    @pl.when(has_high)
    def _():
        v_up.wait_send()
        v_down.wait_recv()

    def halo_split(i, _):
        splits(5 * i, halo[i])
        return 0

    lax.fori_loop(0, 2, halo_split, 0)
    e_low, e_high = edge_copy(1, 0, 1), edge_copy(2, 5, 1)
    e_low.start()
    e_high.start()

    for odd in range(2):
        for place in range(2):
            a = (3, 1, 2, 0)[2 * odd + place]
            block = wts[:, a * taps : (a + 1) * taps].astype(F32)
            wt_t[odd, :, place * n_out : (place + 1) * n_out] = block.T.astype(BF16)

    k_reduce(0)
    e_low.wait()
    e_high.wait()

    def build_halo(i, _):
        build(5 * i)
        return 0

    lax.fori_loop(0, 2, build_halo, 0)

    def forward(step, _):
        d, at = step // (area // 256), step % (area // 256)
        lanes = pl.ds(pl.multiple_of(at * 256, 256), 256)
        block = cols[pl.ds(2 * d, 4), :, :, :, lanes].reshape(4 * taps, 256)
        part = jnp.dot(wts[...], block, preferred_element_type=F32)
        fsum[d, :, lanes] = part
        fsend[d, :, lanes] = part.astype(BF16)
        return 0

    lax.fori_loop(0, 2 * (area // 256), forward, 0)

    def out_rows(ref, owner):
        return ref.at[:, pl.ds(pl.multiple_of(owner * local_out, local_out), local_out), :]

    f_copies = []
    for k in range(1, nx):
        peer = lax.rem(x + k, nx)
        f_copies.append(remote(out_rows(fsend, peer), frecv.at[k - 1], f_send.at[k - 1], f_recv.at[k - 1], {"ch": peer}))
        f_copies[-1].start()

    def outer_parts(index, _):
        kernel_part(1, index, 3 * index)
        return 0

    lax.fori_loop(0, 2, outer_parts, 0)
    k_pair(1).start()

    @pl.when(has_low)
    def _():
        g_down.wait_send()
        g_up.wait_recv()

    @pl.when(has_high)
    def _():
        g_up.wait_send()
        g_down.wait_recv()

    g_edge = remote(
        gbuf.at[:, :, pl.ds(pl.multiple_of(jnp.where(s == 0, area, 128), 128), 128)],
        gbuf.at[:, :, pl.ds(pl.multiple_of(jnp.where(s == 0, 0, 128 + area), 128), 128)],
        ge_sem.at[0], ge_sem.at[1], {"sub": other},
    )
    g_edge.start()

    g_edge.wait_send()
    remote(
        gbuf.at[:, :, pl.ds(0, 128)],
        gbuf.at[:, :, pl.ds(pl.multiple_of(jnp.where(s == 0, 128 + area, 0), 128), 128)],
        ge_sem.at[0], ge_sem.at[1], {"sub": other},
    ).wait_recv()

    lane = lax.broadcasted_iota(jnp.int32, (cin, 128), 1) % 64
    inner_low, inner_high = lane > 0, lane < 63
    weave = (l_at == 2 * (k_at % 64) + k_at // 64).astype(BF16)

    def volume_plane(step, _):
        pl.when(step == 1)(lambda: k_reduce(1))
        i = jnp.where(step < 2, step + 1, 3 * (step - 2))
        block = gbuf[pl.ds((i + 1) // 2, 2)].reshape(2 * n_out, 256 + area)
        wide[...] = jnp.dot(wt_t[i % 2], block, preferred_element_type=F32)

        def term(b, r, t):
            lanes = slice(t * 128, t * 128 + 128)

            def tap(e):
                return wide[(4 * b + e) * cin : (4 * b + e + 1) * cin, lanes]

            if r == 0:
                return tap(1) + jnp.where(inner_low, pltpu.roll(tap(3), 1, 1), 0.0)
            return tap(2) + jnp.where(inner_high, pltpu.roll(tap(0), 127, 1), 0.0)

        for q in range(2):
            kept = [None, None]
            for t in range(1, tiles + 1):
                both = []
                for r in range(2):
                    if q == 0:
                        before = pltpu.roll(term(3, r, t - 1), 64, 1) if kept[r] is None else kept[r]
                        after = pltpu.roll(term(3, r, t), 64, 1)
                        base = term(1, r, t)
                    else:
                        before = pltpu.roll(term(0, r, t), 64, 1) if kept[r] is None else kept[r]
                        after = pltpu.roll(term(0, r, t + 1), 64, 1)
                        base = term(2, r, t)
                    kept[r] = after
                    both.append(base + jnp.where(first, before, after))
                n = 2 * (t - 1)
                rows32[pl.ds(2 * n + q, cin, stride=pitch), :] = jnp.where(first, both[0], pltpu.roll(both[1], 64, 1))
                rows32[pl.ds(2 * n + 2 + q, cin, stride=pitch), :] = jnp.where(first, pltpu.roll(both[0], 64, 1), both[1])
        ready = rows32[...].reshape(cin, pitch, 128)[:, :high].reshape(cin * high, 128)
        woven = jnp.dot(ready.astype(BF16), weave, preferred_element_type=F32)
        vgrad[:, i] = woven.astype(BF16).reshape(cin, high, 128)
        return 0

    lax.fori_loop(0, 4, volume_plane, 0)

    for d in range(2):
        total = fsum[d, pl.ds(pl.multiple_of(x * local_out, local_out), local_out), :]
        for k in range(1, nx):
            if d == 0:
                f_copies[k - 1].wait()
            total = total + frecv[k - 1, d].astype(F32)
        feat[d] = total.astype(BF16)

    for group in range(2):
        result = krecv[group, z]
        for k in range(1, nz):
            k_copy(group, k).wait()
            result = result + kzin[group, k - 1, 0:rows, :].astype(F32)
        for index in range(2):
            a = (1 + index, 3 * index)[group]
            kgrad[:, a * taps : (a + 1) * taps] = result[:, index * taps : (index + 1) * taps]


def body(volume, kernel, cotangent):
    n_out, cin = kernel.shape[:2]
    nz, nx = lax.axis_size("sp"), lax.axis_size("ch")
    local_out, depth, area = cotangent.shape
    high = volume.shape[2]
    rows = n_out // (2 * nz)
    padded_rows = -(-rows // 16) * 16
    weights = kernel.transpose(0, 2, 1).reshape(n_out, 64 * cin)
    grads = cotangent.transpose(1, 0, 2)
    vmem = pl.BlockSpec(memory_space=pltpu.VMEM)
    dma = pltpu.SemaphoreType.DMA
    feat, vgrad, kgrad = pl.pallas_call(
        functools.partial(kernel_body, nz, nx),
        out_shape=(
            jax.ShapeDtypeStruct((depth, local_out, area), BF16),
            jax.ShapeDtypeStruct(volume.shape, BF16),
            jax.ShapeDtypeStruct((rows, 64 * cin), F32),
        ),
        in_specs=[vmem] * 3,
        out_specs=[vmem] * 3,
        scratch_shapes=[
            pltpu.VMEM((2, cin, high, 128), BF16),
            pltpu.VMEM((6, 2, cin * (high + 8), 128), F32),
            pltpu.VMEM((6, 2, cin, 128), BF16),
            pltpu.VMEM((6, 2, cin, 128), BF16),
            pltpu.VMEM((6, 4, 4, cin, area), BF16),
            pltpu.VMEM((4, n_out, 256 + area), BF16),
            pltpu.VMEM((depth, n_out, area), F32),
            pltpu.VMEM((depth, n_out, area), BF16),
            pltpu.VMEM((nx - 1, depth, local_out, area), BF16),
            pltpu.VMEM((2, nz, 2, rows, 32 * cin), F32),
            pltpu.VMEM((2, nz, rows, 32 * cin), F32),
            pltpu.VMEM((2, nz, padded_rows, 32 * cin), BF16),
            pltpu.VMEM((2, nz - 1, padded_rows, 32 * cin), BF16),
            pltpu.VMEM((16 * cin, 256 + area), F32),
            pltpu.VMEM((cin * (high + 8), 128), F32),
            pltpu.VMEM((2, 16 * cin, 2 * n_out), BF16),
            dma((2,)), dma((2,)),
            dma((nx - 1,)), dma((nx - 1,)),
            dma((2,)), dma((2,)),
            dma((3,)), dma((3,)),
            dma((2,)),
            dma((nx - 1,)), dma((nx - 1,)),
            dma((2, 2)),
            dma((2, nz - 1)), dma((2, nz - 1)),
            dma,
        ],
        compiler_params=pltpu.CompilerParams(
            collective_id=0, has_side_effects=True, vmem_limit_bytes=56 * 1024 * 1024
        ),
    )(volume, weights, grads)
    features = feat.transpose(1, 0, 2)
    kernel_grad = kgrad.reshape(rows, 64, cin).transpose(0, 2, 1)
    return (features, vgrad, kernel_grad)


def solution(mesh):
    return jax.shard_map(
        body,
        mesh=mesh,
        in_specs=(
            P("ch", ("grp", "sp"), "sub", None),
            P(None, "ch", None),
            P("ch", ("grp", "sp"), "sub"),
        ),
        out_specs=(
            P("ch", ("grp", "sp"), "sub"),
            P("ch", ("grp", "sp"), "sub", None),
            P(("grp", "sp", "sub"), "ch", None),
        ),
        check_vma=False,
    )
```

time: 48.1 us -> 39.2 us (0.81)
  Pallas kernels: 40 us -> 31.1 us
    pallas_call x1, Pallas kernels: 40 us -> 31.1 us  [body(): pl.pallas_call(functools.partial(kernel_body, nz, nx), out_shape=(jax.Sha...]
where the time goes in v2:
time: 39.2 us; the launch traced here: 39 us
  Pallas kernels  31.1 us (79%)
  local copies, waits for them, and re-layouts  7.21 us (18%)
  between operations  0.68 us (2%)
    pallas_call x1, Pallas kernels, body(): pl.pallas_call(functools.partial(kernel_body, nz, nx), out_shape=(jax.Sha...  31.1 us
    unnamed x11, local copies, waits for them, and re-layouts  5.04 us
    reshape x1, local copies, waits for them, and re-layouts, body(): kernel_grad = kgrad.reshape(rows, 64, cin).transpose(0, 2, 1)  1.16 us
    reshape x1, local copies, waits for them, and re-layouts, body(): weights = kernel.transpose(0, 2, 1).reshape(n_out, 64 * cin)  1.01 us

profile of v2, /device:TPU:0, one launch (start us, length us, event | category | flops | bytes accessed | tf_op | source)
XLA Modules:
  0.0 39.0 jit_solution(10300297515926452329)
XLA Ops:
  0.6 1.4 %copy.10 = bf16[128,32,64]{0,1,2:T(8,128)(2,1)S(1)} copy(bf16[128,32,64]{0,2,1:T(8,128)(2,1)} %param.4) | data formatting | bytes 1048576 | tf_op args[1]
  2.0 0.0 copy-start.1
  2.0 1.0 %copy.12.wts = bf16[128,2048]{1,0:T(8,128)(2,1)} copy(bf16[128,2048]{0,1:T(8,128)(2,1)S(1)} %bitcast.9) | data formatting | bytes 1048576 | tf_op jit(solution)/shard_map/reshape | solution.py:360
  3.0 0.0 copy-done.1
  3.0 0.8 %copy.16 = bf16[64,2,1024]{2,0,1:T(8,128)(2,1)} copy(bf16[64,2,1024]{2,1,0:T(2,128)(2,1)S(1)} %copy-done.1) | data formatting | bytes 524288 | tf_op args[2]
  3.8 31.1 %shard_map.58 = (bf16[2,64,1024]{2,1,0:T(8,128)(2,1)}, bf16[32,4,32,128]{3,2,1,0:T(8,128)(2,1)}, f32[16,2048]{1,0:T(8,128)}) custom-call(bf16[32,4,32,128]{3,2,1,0:T(8,128)(2,1)} %vol.1, bf16[128,2048]{1,0:T(8,128)(2,1)} %copy.12.wts, bf16[2,64,1024]{2,1,0:T(8,128)(2,1)} %bitcast.10), custom_call_target="tpu_custom_call" | custom-call | tf_op jit(solution)/shard_map/pallas_call | solution.py:364
  34.9 0.0 copy-start
  34.9 1.2 %reshape.13 = f32[16,64,32]{2,1,0:T(8,128)S(1)} reshape(f32[16,2048]{1,0:T(8,128)} %get-tuple-element.8) | data formatting | bytes 262144 | tf_op jit(solution)/shard_map/reshape | solution.py:405
  36.1 0.0 copy-start.2
  36.1 0.9 %copy.14 = f32[16,32,64]{2,1,0:T(8,128)} copy(f32[16,32,64]{1,2,0:T(8,128)S(1)} %bitcast.8) | data formatting | bytes 262144
  37.0 0.0 copy-done.2
  37.0 1.0 %copy.13 = bf16[64,2,1024]{2,1,0:T(2,128)(2,1)} copy(bf16[64,2,1024]{2,0,1:T(8,128)(2,1)S(1)} %bitcast.11) | data formatting | bytes 524288
  38.0 0.0 copy-done
  38.0 1.0 %copy.18 = bf16[32,4,32,128]{3,2,1,0:T(8,128)(2,1)} copy(bf16[32,4,32,128]{3,2,1,0:T(8,128)(2,1)S(1)} %copy-done) | data formatting | bytes 2097152
Async XLA Ops:
  2.0 1.0 %copy-start.1 = (bf16[64,2,1024]{2,1,0:T(2,128)(2,1)S(1)}, bf16[64,2,1024]{2,1,0:T(2,128)(2,1)}, u32[]{:S(2)}) copy-start(bf16[64,2,1024]{2,1,0:T(2,128)(2,1)} %param.5) | copy-start | bytes 786436
  34.9 3.1 %copy-start = (bf16[32,4,32,128]{3,2,1,0:T(8,128)(2,1)S(1)}, bf16[32,4,32,128]{3,2,1,0:T(8,128)(2,1)}, u32[]{:S(2)}) copy-start(bf16[32,4,32,128]{3,2,1,0:T(8,128)(2,1)} %get-tuple-element.19) | copy-start | bytes 3145732
  36.1 1.0 %copy-start.2 = (bf16[2,64,1024]{2,1,0:T(8,128)(2,1)S(1)}, bf16[2,64,1024]{2,1,0:T(8,128)(2,1)}, u32[]{:S(2)}) copy-start(bf16[2,64,1024]{2,1,0:T(8,128)(2,1)} %get-tuple-element.6) | copy-start | bytes 786436

commit v3 on v2

--- a/solution.py
+++ b/solution.py
@@ -14,7 +14,7 @@
 
 def kernel_body(
     nz, nx, vol, wts, cot, feat, vgrad, kgrad,
-    halo, split, edge_out, edge_in, cols, gbuf, fsum, fsend, frecv, kpart, krecv, ksend, kzin, wide, rows32, wt_t,
+    halo, split, edge_out, edge_in, cols, gbuf, fsum, fsend, frecv, kpart, krecv, ksend, kzin, wide, rows32, wt_t, wt, wrows,
     v_send, v_recv, g_send, g_recv, gz_send, gz_recv, e_send, e_recv, ge_sem, f_send, f_recv, ks_sem, kz_send, kz_recv, own_sem,
 ):
     z = lax.axis_index("sp")
@@ -23,7 +23,7 @@
     other = 1 - s
     cin = vol.shape[0]
     high = vol.shape[2]
-    n_out = wts.shape[0]
+    n_out = wts.shape[2]
     local_out = cot.shape[1]
     area = cot.shape[2]
     tiles = area // 128
@@ -111,6 +111,18 @@
     e_own = edge_copy(0, 1, 4)
     e_own.start()
 
+    step = 64 + 8
+    for c in range(cin):
+        wrows[c * step : c * step + 64, :] = wts[c].astype(F32)
+    for tap in range(64):
+        odd, place = ((1, 1), (0, 1), (1, 0), (0, 0))[tap // 16]
+        block = wrows[pl.ds(tap, cin, stride=step), :]
+        wt_t[odd, (tap % 16) * cin : (tap % 16 + 1) * cin, place * n_out : (place + 1) * n_out] = block.astype(BF16)
+    for a in range(4):
+        odd, place = ((1, 1), (0, 1), (1, 0), (0, 0))[a]
+        block = wt_t[odd, :, place * n_out : (place + 1) * n_out].astype(F32)
+        wt[:, a * taps : (a + 1) * taps] = block.T.astype(BF16)
+
     def build(plane):
         for half in range(2):
             rim = edge_in[plane, half].astype(F32)
@@ -141,6 +153,43 @@
 
     g_down = remote(g_plane(1), g_plane(3), gz_send.at[0], gz_recv.at[1], {"sp": low})
     g_up = remote(g_plane(2), g_plane(0), gz_send.at[1], gz_recv.at[0], {"sp": up})
+    def rim_lanes(at):
+        return pl.ds(pl.multiple_of(at, 128), 128)
+
+    def g_edge(index, start, count):
+        planes = pl.ds(start, count)
+        return remote(
+            gbuf.at[planes, :, rim_lanes(jnp.where(s == 0, area, 128))],
+            gbuf.at[planes, :, rim_lanes(jnp.where(s == 0, 0, 128 + area))],
+            ge_sem.at[0, index], ge_sem.at[1, index], {"sub": other},
+        )
+
+    def g_edge_wait(index, start, count):
+        planes = pl.ds(start, count)
+        g_edge(index, start, count).wait_send()
+        remote(
+            gbuf.at[planes, :, rim_lanes(jnp.where(s == 0, area, 128))],
+            gbuf.at[planes, :, rim_lanes(jnp.where(s == 0, 128 + area, 0))],
+            ge_sem.at[0, index], ge_sem.at[1, index], {"sub": other},
+        ).wait_recv()
+
+    def outer_planes():
+        @pl.when(has_low)
+        def _():
+            g_down.wait_send()
+            g_up.wait_recv()
+
+        @pl.when(has_high)
+        def _():
+            g_up.wait_send()
+            g_down.wait_recv()
+        g_edge(1, 0, 1).start()
+        g_edge(2, 3, 1).start()
+
+    def outer_rims():
+        g_edge_wait(1, 0, 1)
+        g_edge_wait(2, 3, 1)
+
     def spread():
         own.wait()
         for k in range(1, nx):
@@ -149,9 +198,10 @@
             remote(cot, g_rows(origin), g_send.at[k - 1], g_recv.at[k - 1], {"ch": origin}).wait_recv()
         pl.when(has_low)(g_down.start)
         pl.when(has_high)(g_up.start)
+        g_edge(0, 1, 2).start()
 
     def build_own(i, _):
-        pl.when(i == 2)(spread)
+        pl.when(i == 3)(spread)
         build(i + 1)
         return 0
 
@@ -220,12 +270,6 @@
     e_low.start()
     e_high.start()
 
-    for odd in range(2):
-        for place in range(2):
-            a = (3, 1, 2, 0)[2 * odd + place]
-            block = wts[:, a * taps : (a + 1) * taps].astype(F32)
-            wt_t[odd, :, place * n_out : (place + 1) * n_out] = block.T.astype(BF16)
-
     k_reduce(0)
     e_low.wait()
     e_high.wait()
@@ -235,12 +279,13 @@
         return 0
 
     lax.fori_loop(0, 2, build_halo, 0)
+
 
     def forward(step, _):
         d, at = step // (area // 256), step % (area // 256)
         lanes = pl.ds(pl.multiple_of(at * 256, 256), 256)
         block = cols[pl.ds(2 * d, 4), :, :, :, lanes].reshape(4 * taps, 256)
-        part = jnp.dot(wts[...], block, preferred_element_type=F32)
+        part = jnp.dot(wt[...], block, preferred_element_type=F32)
         fsum[d, :, lanes] = part
         fsend[d, :, lanes] = part.astype(BF16)
         return 0
@@ -263,29 +308,8 @@
     lax.fori_loop(0, 2, outer_parts, 0)
     k_pair(1).start()
 
-    @pl.when(has_low)
-    def _():
-        g_down.wait_send()
-        g_up.wait_recv()
-
-    @pl.when(has_high)
-    def _():
-        g_up.wait_send()
-        g_down.wait_recv()
-
-    g_edge = remote(
-        gbuf.at[:, :, pl.ds(pl.multiple_of(jnp.where(s == 0, area, 128), 128), 128)],
-        gbuf.at[:, :, pl.ds(pl.multiple_of(jnp.where(s == 0, 0, 128 + area), 128), 128)],
-        ge_sem.at[0], ge_sem.at[1], {"sub": other},
-    )
-    g_edge.start()
-
-    g_edge.wait_send()
-    remote(
-        gbuf.at[:, :, pl.ds(0, 128)],
-        gbuf.at[:, :, pl.ds(pl.multiple_of(jnp.where(s == 0, 128 + area, 0), 128), 128)],
-        ge_sem.at[0], ge_sem.at[1], {"sub": other},
-    ).wait_recv()
+
+    g_edge_wait(0, 1, 2)
 
     lane = lax.broadcasted_iota(jnp.int32, (cin, 128), 1) % 64
     inner_low, inner_high = lane > 0, lane < 63
@@ -293,6 +317,8 @@
 
     def volume_plane(step, _):
         pl.when(step == 1)(lambda: k_reduce(1))
+        pl.when(step == 1)(outer_planes)
+        pl.when(step == 2)(outer_rims)
         i = jnp.where(step < 2, step + 1, 3 * (step - 2))
         block = gbuf[pl.ds((i + 1) // 2, 2)].reshape(2 * n_out, 256 + area)
         wide[...] = jnp.dot(wt_t[i % 2], block, preferred_element_type=F32)
@@ -357,7 +383,7 @@
     high = volume.shape[2]
     rows = n_out // (2 * nz)
     padded_rows = -(-rows // 16) * 16
-    weights = kernel.transpose(0, 2, 1).reshape(n_out, 64 * cin)
+    weights = kernel.transpose(1, 2, 0)
     grads = cotangent.transpose(1, 0, 2)
     vmem = pl.BlockSpec(memory_space=pltpu.VMEM)
     dma = pltpu.SemaphoreType.DMA
@@ -387,11 +413,13 @@
             pltpu.VMEM((16 * cin, 256 + area), F32),
             pltpu.VMEM((cin * (high + 8), 128), F32),
             pltpu.VMEM((2, 16 * cin, 2 * n_out), BF16),
+            pltpu.VMEM((n_out, 64 * cin), BF16),
+            pltpu.VMEM((cin * (64 + 8), n_out), F32),
             dma((2,)), dma((2,)),
             dma((nx - 1,)), dma((nx - 1,)),
             dma((2,)), dma((2,)),
             dma((3,)), dma((3,)),
-            dma((2,)),
+            dma((2, 3)),
             dma((nx - 1,)), dma((nx - 1,)),
             dma((2, 2)),
             dma((2, nz - 1)), dma((2, nz - 1)),

time: 39.2 us -> 36.7 us (0.936)
  local copies, waits for them, and re-layouts: 7.21 us -> 5.75 us
  Pallas kernels: 31.1 us -> 30 us
    pallas_call x1, Pallas kernels: 31.1 us -> 30 us  [body(): pl.pallas_call(functools.partial(kernel_body, nz, nx), out_shape=(jax.Sha...]
    reshape x1 -> x0, local copies, waits for them, and re-layouts: 1.01 us -> none  [body(): weights = kernel.transpose(0, 2, 1).reshape(n_out, 64 * cin)]
    unnamed x11 -> x8, local copies, waits for them, and re-layouts: 5.04 us -> 4.59 us
where the time goes in v3:
time: 36.7 us; the launch traced here: 36.5 us
  Pallas kernels  30 us (82%)
  local copies, waits for them, and re-layouts  5.75 us (16%)
  between operations  0.66 us (2%)
    pallas_call x1, Pallas kernels, body(): pl.pallas_call(functools.partial(kernel_body, nz, nx), out_shape=(jax.Sha...  30 us
    unnamed x8, local copies, waits for them, and re-layouts  4.59 us
    reshape x1, local copies, waits for them, and re-layouts, body(): kernel_grad = kgrad.reshape(rows, 64, cin).transpose(0, 2, 1)  1.16 us

profile of v3, /device:TPU:0, one launch (start us, length us, event | category | flops | bytes accessed | tf_op | source)
XLA Modules:
  0.0 36.5 jit_solution(4837631465048643328)
XLA Ops:
  0.6 1.7 %copy.13 = bf16[64,2,1024]{2,0,1:T(8,128)(2,1)} copy(bf16[64,2,1024]{2,1,0:T(2,128)(2,1)} %param.5) | data formatting | bytes 524288 | tf_op args[2]
  2.3 30.0 %shard_map.58 = (bf16[2,64,1024]{2,1,0:T(8,128)(2,1)}, bf16[32,4,32,128]{3,2,1,0:T(8,128)(2,1)}, f32[16,2048]{1,0:T(8,128)}) custom-call(bf16[32,4,32,128]{3,2,1,0:T(8,128)(2,1)} %vol.1, bf16[32,64,128]{2,1,0:T(8,128)(2,1)} %bitcast.8, bf16[2,64,1024]{2,1,0:T(8,128)(2,1)} %bitcast.7), custom_call_target="tpu_custom_call" | custom-call | tf_op jit(solution)/shard_map/pallas_call | solution.py:390
  32.4 0.0 copy-start
  32.4 1.2 %reshape.9 = f32[16,64,32]{2,1,0:T(8,128)S(1)} reshape(f32[16,2048]{1,0:T(8,128)} %get-tuple-element.8) | data formatting | bytes 262144 | tf_op jit(solution)/shard_map/reshape | solution.py:433
  33.6 0.0 copy-start.1
  33.6 0.9 %copy.11 = f32[16,32,64]{2,1,0:T(8,128)} copy(f32[16,32,64]{1,2,0:T(8,128)S(1)} %bitcast.6) | data formatting | bytes 262144
  34.5 0.0 copy-done.1
  34.5 1.0 %copy.10 = bf16[64,2,1024]{2,1,0:T(2,128)(2,1)} copy(bf16[64,2,1024]{2,0,1:T(8,128)(2,1)S(1)} %bitcast.9) | data formatting | bytes 524288
  35.5 0.0 copy-done
  35.5 1.0 %copy.15 = bf16[32,4,32,128]{3,2,1,0:T(8,128)(2,1)} copy(bf16[32,4,32,128]{3,2,1,0:T(8,128)(2,1)S(1)} %copy-done) | data formatting | bytes 2097152
Async XLA Ops:
  32.4 3.1 %copy-start = (bf16[32,4,32,128]{3,2,1,0:T(8,128)(2,1)S(1)}, bf16[32,4,32,128]{3,2,1,0:T(8,128)(2,1)}, u32[]{:S(2)}) copy-start(bf16[32,4,32,128]{3,2,1,0:T(8,128)(2,1)} %get-tuple-element.19) | copy-start | bytes 3145732
  33.6 1.0 %copy-start.1 = (bf16[2,64,1024]{2,1,0:T(8,128)(2,1)S(1)}, bf16[2,64,1024]{2,1,0:T(8,128)(2,1)}, u32[]{:S(2)}) copy-start(bf16[2,64,1024]{2,1,0:T(8,128)(2,1)} %get-tuple-element.6) | copy-start | bytes 786436

commit v4 on v3

--- a/solution.py
+++ b/solution.py
@@ -316,8 +316,8 @@
     weave = (l_at == 2 * (k_at % 64) + k_at // 64).astype(BF16)
 
     def volume_plane(step, _):
+        pl.when(step == 1)(outer_planes)
         pl.when(step == 1)(lambda: k_reduce(1))
-        pl.when(step == 1)(outer_planes)
         pl.when(step == 2)(outer_rims)
         i = jnp.where(step < 2, step + 1, 3 * (step - 2))
         block = gbuf[pl.ds((i + 1) // 2, 2)].reshape(2 * n_out, 256 + area)

time: 36.7 us -> 36.7 us (level)
  no operation moved by 1% of the time
where the time goes in v4:
time: 36.7 us; the launch traced here: 36.5 us
  Pallas kernels  30 us (82%)
  local copies, waits for them, and re-layouts  5.75 us (16%)
  between operations  0.66 us (2%)
    pallas_call x1, Pallas kernels, body(): pl.pallas_call(functools.partial(kernel_body, nz, nx), out_shape=(jax.Sha...  30 us
    unnamed x8, local copies, waits for them, and re-layouts  4.59 us
    reshape x1, local copies, waits for them, and re-layouts, body(): kernel_grad = kgrad.reshape(rows, 64, cin).transpose(0, 2, 1)  1.16 us

profile of v4, /device:TPU:0, one launch (start us, length us, event | category | flops | bytes accessed | tf_op | source)
XLA Modules:
  0.0 36.5 jit_solution(14502354842363663645)
XLA Ops:
  0.6 1.7 %copy.13 = bf16[64,2,1024]{2,0,1:T(8,128)(2,1)} copy(bf16[64,2,1024]{2,1,0:T(2,128)(2,1)} %param.5) | data formatting | bytes 524288 | tf_op args[2]
  2.3 30.0 %shard_map.58 = (bf16[2,64,1024]{2,1,0:T(8,128)(2,1)}, bf16[32,4,32,128]{3,2,1,0:T(8,128)(2,1)}, f32[16,2048]{1,0:T(8,128)}) custom-call(bf16[32,4,32,128]{3,2,1,0:T(8,128)(2,1)} %vol.1, bf16[32,64,128]{2,1,0:T(8,128)(2,1)} %bitcast.8, bf16[2,64,1024]{2,1,0:T(8,128)(2,1)} %bitcast.7), custom_call_target="tpu_custom_call" | custom-call | tf_op jit(solution)/shard_map/pallas_call | solution.py:390
  32.4 0.0 copy-start
  32.4 1.2 %reshape.9 = f32[16,64,32]{2,1,0:T(8,128)S(1)} reshape(f32[16,2048]{1,0:T(8,128)} %get-tuple-element.8) | data formatting | bytes 262144 | tf_op jit(solution)/shard_map/reshape | solution.py:433
  33.6 0.0 copy-start.1
  33.6 0.9 %copy.11 = f32[16,32,64]{2,1,0:T(8,128)} copy(f32[16,32,64]{1,2,0:T(8,128)S(1)} %bitcast.6) | data formatting | bytes 262144
  34.5 0.0 copy-done.1
  34.5 1.0 %copy.10 = bf16[64,2,1024]{2,1,0:T(2,128)(2,1)} copy(bf16[64,2,1024]{2,0,1:T(8,128)(2,1)S(1)} %bitcast.9) | data formatting | bytes 524288
  35.5 0.0 copy-done
  35.5 1.0 %copy.15 = bf16[32,4,32,128]{3,2,1,0:T(8,128)(2,1)} copy(bf16[32,4,32,128]{3,2,1,0:T(8,128)(2,1)S(1)} %copy-done) | data formatting | bytes 2097152
Async XLA Ops:
  32.4 3.1 %copy-start = (bf16[32,4,32,128]{3,2,1,0:T(8,128)(2,1)S(1)}, bf16[32,4,32,128]{3,2,1,0:T(8,128)(2,1)}, u32[]{:S(2)}) copy-start(bf16[32,4,32,128]{3,2,1,0:T(8,128)(2,1)} %get-tuple-element.19) | copy-start | bytes 3145732
  33.6 1.0 %copy-start.1 = (bf16[2,64,1024]{2,1,0:T(8,128)(2,1)S(1)}, bf16[2,64,1024]{2,1,0:T(8,128)(2,1)}, u32[]{:S(2)}) copy-start(bf16[2,64,1024]{2,1,0:T(8,128)(2,1)} %get-tuple-element.6) | copy-start | bytes 786436
